TPU v7x, 32 devices: a whole 2x2x4 slice. The times are simulated.
32 devices in a mesh: groups: 2 (over y), expert: 8 (over z, x), dp: 2 (over core).
Axes of the slice: x: 2, y: 2, z: 4, core: 2. Of those that a mesh axis runs over, the one named last changes fastest.
Arguments:
- out_grad: bfloat16 [4096, 1280], P(('groups', 'expert', 'dp')), parts along dimension 0, may hold values from -6 to 6
- gates: bfloat16 [4096, 6], P(('groups', 'expert', 'dp')), parts along dimension 0, may hold values from 0.099609375 to 1
- routes: int32 [4096, 6], P(('groups', 'expert', 'dp')), parts along dimension 0, may hold values from 0 to 63, all different within a row; in each aligned block of 128 rows (0 to 127, 128 to 255, ...) at most 14 rows name the same one
- tile_slot: int32 [4096], P(('groups', 'expert', 'dp')), parts along dimension 0, may hold values from -1 to 127, as said below
- w_in: bfloat16 [64, 1280, 768], P('expert', 'dp'), may hold values from -0.15625 to 0.15625
- w_out: bfloat16 [64, 768, 1280], P('expert', None, 'dp'), may hold values from -0.21875 to 0.21875
- expert_pre: bfloat16 [256, 8, 14, 768], P(('groups', 'expert', 'dp')), parts along dimension 0, may hold values from -6 to 6
- adapter_pre: bfloat16 [2048, 1280], P(('groups', 'expert', 'dp')), parts along dimension 0, may hold values from -6 to 6
- w_adapt: bfloat16 [2304, 1280], P(('expert', 'dp')), may hold values from -0.125 to 0.125
Outputs:
- token_grads: bfloat16 [4096, 1280], P(('groups', 'expert', 'dp')), parts along dimension 0
- patch_grads: float32 [512, 9216], P(('groups', 'expert', 'dp')), parts along dimension 0
There are 2 independent parts, one for each index of `groups`. A program takes and returns all parts, laid end to end along the dimension named above; an argument that names none is the same for every part. Nothing has to cross between parts.
Inputs may be any that keep to these rules, and one draw needn't show every extreme that they name: `routes`: in each aligned block of 128 rows (the tokens of one device) no expert is named by more than 14 rows, a bound that some block reaches. `tile_slot`: -1 marks a text token. In each aligned block of 256 tokens every value 0 to 127 appears exactly once; value v belongs to slot v mod 64 of the (v div 64)-th device of the block.
All inputs are finite; a program needn't handle non-finite values.
Results may differ from a plain program's by a relative error of at most 0.0064.
Values may be sent and summed in bfloat16 or wider, within the bound.
A program may use at most 128 MiB of HBM per device.

v0:
```python
import jax
import jax.numpy as jnp
from jax import lax
from jax.sharding import PartitionSpec as P

EXPERTS = 64
SIGW = 576
TILE_R = 8


def silu_slope(value):
    sigma = jax.nn.sigmoid(value)
    return sigma * (1.0 + value * (1.0 - sigma))


def gelu_slope(value):
    normal_cdf = 0.5 * (1.0 + lax.erf(value * 0.7071067811865476))
    return normal_cdf + value * jnp.exp(-0.5 * value * value) * 0.3989422804014327


def body(out_grad, gates, routes, tile_slot, w_in, w_out, expert_pre, adapter_pre, w_adapt):
    axis_count = lax.axis_size("expert")
    core_count = lax.axis_size("dp")
    tok_count, feature_width = out_grad.shape
    top_count = routes.shape[1]
    local_experts = w_in.shape[0]
    replicas = max(1, axis_count // EXPERTS)
    slot_depth = expert_pre.shape[2]
    slot_total = axis_count * local_experts * slot_depth
    flat_routes = routes.reshape(-1)
    expert_hot = (flat_routes[:, None] == jnp.arange(EXPERTS, dtype=jnp.int32)[None, :]).astype(
        jnp.int32
    )
    earlier = jnp.cumsum(expert_hot, axis=0) - expert_hot
    row_rank = jnp.sum(earlier * expert_hot, axis=1)
    slot_range = jnp.arange(slot_total, dtype=jnp.int32)[None, :]
    row_hits = jnp.zeros((tok_count * top_count, slot_total), jnp.bool_)
    for piece in range(replicas):
        slot_id = (flat_routes + piece * EXPERTS) * slot_depth + row_rank
        row_hits = jnp.logical_or(row_hits, slot_id[:, None] == slot_range)
    token_slot = row_hits.reshape(tok_count, top_count, slot_total)
    placing = jnp.sum(token_slot.astype(jnp.bfloat16), axis=1)
    gate_slot = jnp.sum(
        jnp.where(token_slot, gates.astype(jnp.float32)[:, :, None], 0.0), axis=(0, 1)
    ).astype(jnp.bfloat16)
    send_rows = lax.dot_general(
        placing, out_grad, (((0,), (0,)), ((), ())), preferred_element_type=jnp.float32
    )
    send_rows = send_rows.astype(jnp.bfloat16).reshape(
        axis_count, local_experts, slot_depth, feature_width
    )
    gate_slot = gate_slot.reshape(axis_count, local_experts, slot_depth)
    recv_rows, recv_gates = (
        lax.all_to_all(send_rows, "expert", split_axis=0, concat_axis=0, tiled=True),
        lax.all_to_all(gate_slot, "expert", split_axis=0, concat_axis=0, tiled=True),
    )
    full_in, full_out = (
        lax.all_gather(w_in, "dp", axis=1, tiled=True),
        lax.all_gather(w_out, "dp", axis=2, tiled=True),
    )
    hidden_grad = jnp.einsum(
        "nlcd,lfd->nlcf", recv_rows, full_out, preferred_element_type=jnp.float32
    )
    hidden_grad = (
        hidden_grad
        * recv_gates.astype(jnp.float32)[..., None]
        * silu_slope(expert_pre.astype(jnp.float32))
    )
    hidden_grad = hidden_grad.astype(jnp.bfloat16)
    row_grad = jnp.einsum(
        "nlcf,ldf->nlcd", hidden_grad, full_in, preferred_element_type=jnp.float32
    ).astype(jnp.bfloat16)
    returned = lax.all_to_all(row_grad, "expert", split_axis=0, concat_axis=0, tiled=True)
    token_grads = jnp.dot(
        placing, returned.reshape(slot_total, feature_width), preferred_element_type=jnp.float32
    ).astype(jnp.bfloat16)
    vis_count = adapter_pre.shape[0]
    owner_hot = (
        tile_slot[None, :] == jnp.arange(core_count * vis_count, dtype=jnp.int32)[:, None]
    ).astype(jnp.bfloat16)
    outgoing = jnp.dot(owner_hot, token_grads, preferred_element_type=jnp.float32).astype(
        jnp.bfloat16
    )
    incoming = lax.all_to_all(
        outgoing.reshape(core_count, vis_count, feature_width),
        "dp",
        split_axis=0,
        concat_axis=0,
        tiled=True,
    )
    visual_grad = jnp.sum(incoming.astype(jnp.float32), axis=0)
    adapter_grad = (visual_grad * gelu_slope(adapter_pre.astype(jnp.float32))).astype(jnp.bfloat16)
    shuffled = lax.dot_general(
        adapter_grad,
        lax.all_gather(w_adapt, ("expert", "dp"), axis=0, tiled=True),
        (((1,), (1,)), ((), ())),
        preferred_element_type=jnp.float32,
    )
    tile_cols = vis_count // TILE_R
    patch_grads = shuffled.reshape(TILE_R, tile_cols, 2, 2, SIGW).transpose(0, 2, 1, 3, 4)
    patch_grads = patch_grads.reshape(2 * TILE_R, 2 * tile_cols * SIGW)
    return (token_grads, patch_grads)


def solution(mesh):
    placed = (
        P(("groups", "expert", "dp"), None),
        P(("groups", "expert", "dp"), None),
        P(("groups", "expert", "dp"), None),
        P(("groups", "expert", "dp")),
        P("expert", "dp", None),
        P("expert", None, "dp"),
        P(("groups", "expert", "dp"), None, None, None),
        P(("groups", "expert", "dp"), None),
        P(("expert", "dp"), None),
    )
    return jax.shard_map(
        body,
        mesh=mesh,
        in_specs=placed,
        out_specs=(P(("groups", "expert", "dp"), None), P(("groups", "expert", "dp"), None)),
        check_vma=False,
    )
```

profile of v0, /device:TPU:0, one launch (start us, length us, event | category | flops | bytes accessed | tf_op | source)
XLA Modules:
  0.0 203.0 jit_solution(8682341651124602853)
XLA Ops:
  7.2 0.0 copy-start
  7.2 0.0 all-gather.4.cloned.1.call-start
  7.2 0.7 all-gather.4.cloned.1.call-update
  7.9 0.0 copy-start.4
  7.9 0.0 copy-start.5
  7.9 0.0 all-gather.6.cloned.1.call-start
  8.0 0.7 all-gather.6.cloned.1.call-update
  8.7 0.0 copy-done.4
  8.7 0.1 copy.51
  8.8 0.1 eq.56
  8.9 0.1 eq.52
  9.1 1.8 reduce-window.6
  10.9 0.3 slice_reduce_fusion
  11.2 0.1 fusion.34
  11.4 0.1 reduce_sum.42
  11.5 0.1 copy.54
  11.6 0.0 copy-done.5
  11.6 0.4 select_reduce_fusion
  12.0 0.8 convert_element_type.62
  12.7 7.3 %all-to-all-start.1 = ((bf16[8,8,14]{2,1,0:T(8,128)(2,1)}), bf16[8,8,14]{2,1,0:T(8,128)(2,1)S(1)}, u32[]{:S(2)}, u32[]{:S(2)}) async-start(bf16[8,8,14]{2,1,0:T(8,128)(2,1)} %convert_element_type.62), calls=%async_computation.1 | async-start | bytes 32768 | tf_op jit(solution)/shard_map/all_to_all | solution.py:55
  20.0 0.4 fusion.23
  20.4 2.5 %convolution_convert_fusion = bf16[896,1280]{1,0:T(8,128)(2,1)} fusion(bf16[128,896]{1,0:T(8,128)(2,1)S(1)} %fusion.23, bf16[128,1280]{1,0:T(8,128)(2,1)S(1)} %copy-done), kind=kOutput, calls=%fused_computation.7 | convolution fusion | flops 294748160 | bytes 2850816 | tf_op jit(solution)/shard_map/dot_general | solution.py:46
  22.9 3.1 %reshape.61 = bf16[8,8,14,1280]{3,2,1,0:T(8,128)(2,1)S(1)} reshape(bf16[896,1280]{1,0:T(8,128)(2,1)} %convolution_convert_fusion) | data formatting | bytes 4587520 | tf_op jit(solution)/shard_map/reshape | solution.py:49
  26.0 2.1 %copy.55 = bf16[8,8,14,1280]{3,1,2,0:T(8,128)(2,1)} copy(bf16[8,8,14,1280]{3,2,1,0:T(8,128)(2,1)S(1)} %reshape.61) | data formatting | bytes 4587520 | tf_op jit(solution)/shard_map/reshape | solution.py:49
  28.1 0.0 all-to-all-done.1
  28.1 6.0 %all-to-all-start = ((bf16[8,8,14,1280]{3,1,2,0:T(8,128)(2,1)}), bf16[8,8,14,1280]{3,1,2,0:T(8,128)(2,1)S(1)}, u32[]{:S(2)}, u32[]{:S(2)}) async-start(bf16[8,8,14,1280]{3,1,2,0:T(8,128)(2,1)} %copy.55), calls=%async_computation | async-start | bytes 4587520 | tf_op jit(solution)/shard_map/all_to_all | solution.py:54
  34.1 0.0 all-gather.8.cloned.1.call-start
  34.2 0.7 all-gather.8.cloned.1.call-update
  34.9 51.2 %all-to-all-done = bf16[8,8,14,1280]{3,1,2,0:T(8,128)(2,1)S(1)} async-done(((bf16[8,8,14,1280]{3,1,2,0:T(8,128)(2,1)}), bf16[8,8,14,1280]{3,1,2,0:T(8,128)(2,1)S(1)}, u32[]{:S(2)}, u32[]{:S(2)}) %all-to-all-start) | async-done | bytes 2293792 | tf_op jit(solution)/shard_map/all_to_all | solution.py:54
  86.1 12.2 %fusion.16 = bf16[8,8,14,768]{3,2,0,1:T(8,128)(2,1)} fusion(bf16[8,768,1280]{2,1,0:T(8,128)(2,1)} %all-gather.4.cloned.1.call-done, bf16[8,8,14,1280]{3,1,2,0:T(8,128)(2,1)S(1)} %all-to-all-done, bf16[8,8,14,768]{3,1,2,0:T(8,128)(2,1)} %param.15, f32[8,8,14]{2,0,1:T(8,128)S(1)} %copy.57), kind=kOutput, calls=%fused_computation.15 | convolution fusion | flops 1769177088 | bytes 20778496 | tf_op jit(solution)/shard_map/nlcd,lfd->nlcf/dot_general | solution.py:61
  98.4 11.1 %fusion.7 = bf16[8,8,14,1280]{3,2,0,1:T(8,128)(2,1)S(1)} fusion(bf16[8,8,14,768]{3,2,0,1:T(8,128)(2,1)} %fusion.16, bf16[8,1280,768]{2,1,0:T(8,128)(2,1)} %all-gather.6.cloned.1.call-done), kind=kOutput, calls=%fused_computation.8 | convolution fusion | flops 1762754560 | bytes 19398656 | tf_op jit(solution)/shard_map/nlcf,ldf->nlcd/dot_general | solution.py:70
  109.4 1.3 copy.59
  110.7 69.7 %all_to_all.20 = bf16[8,8,14,1280]{3,1,2,0:T(8,128)(2,1)S(1)} all-to-all(bf16[8,8,14,1280]{3,1,2,0:T(8,128)(2,1)S(1)} %copy.59), channel_id=1, replica_groups=mesh['groups'=2,'expert'=8,'dp'=2] {'expert'}, dimensions={0} | all-to-all | bytes 4587520 | tf_op jit(solution)/shard_map/all_to_all | solution.py:73
  180.4 0.5 copy.60
  180.9 0.0 copy-start.6
  180.9 2.2 %reshape.62 = bf16[896,1280]{1,0:T(8,128)(2,1)} reshape(bf16[8,8,14,1280]{3,2,1,0:T(8,128)(2,1)S(1)} %copy.60) | data formatting | bytes 4587520 | tf_op jit(solution)/shard_map/reshape | solution.py:75
  183.1 2.2 %convolution_convert_fusion.2 = bf16[128,1280]{1,0:T(8,128)(2,1)S(1)} fusion(bf16[128,896]{1,0:T(8,128)(2,1)S(1)} %fusion.23, bf16[896,1280]{1,0:T(8,128)(2,1)} %reshape.62), kind=kOutput, calls=%fused_computation.22 | convolution fusion | flops 293765120 | bytes 2850816 | tf_op jit(solution)/shard_map/dot_general | solution.py:74
  185.3 0.0 copy-start.2
  185.3 0.2 convolution_convert_fusion.1
  185.6 4.0 %all_to_all.21 = bf16[2,64,1280]{2,1,0:T(8,128)(2,1)S(1)} all-to-all(bf16[2,64,1280]{2,1,0:T(8,128)(2,1)S(1)} %bitcast.52), channel_id=1, replica_groups=mesh['groups'=2,'expert'=8,'dp'=2] {'dp'}, dimensions={0} | all-to-all | bytes 655360 | tf_op jit(solution)/shard_map/all_to_all | solution.py:84
  189.6 0.0 all-gather.8.cloned.1.call-done
  189.7 0.0 copy-start.1
  189.7 4.6 %fusion.36 = f32[64,2304]{1,0:T(8,128)S(1)} fusion(bf16[2304,1280]{1,0:T(8,128)(2,1)} %all-gather.8.cloned.1.call-done, f32[64,1280]{1,0:T(8,128)S(1)} %convert_reduce_fusion, bf16[64,1280]{1,0:T(8,128)(2,1)S(1)} %copy-done.3), kind=kOutput, calls=%fused_computation.46 | convolution fusion | flops 378388480 | bytes 6979584 | tf_op jit(solution)/shard_map/dot_general | solution.py:93
  194.3 0.0 copy-done.2
  194.3 0.5 reshape.64
  194.8 0.1 copy.61
  194.9 1.5 reshape.65
  196.4 0.0 copy-done.1
  (12 shorter events, 0.1 us)
Async XLA Ops:
  7.2 13.2 %copy-start = (bf16[128,1280]{1,0:T(8,128)(2,1)S(1)}, bf16[128,1280]{1,0:T(8,128)(2,1)}, u32[]{:S(2)}) copy-start(bf16[128,1280]{1,0:T(8,128)(2,1)} %param.9) | copy-start | bytes 983044
  7.2 78.9 %all-gather.4.cloned.1.call-start = ((), (), s32[]{:S(2)}) async-start(), calls=%async_computation.4 | async-start | bytes 23592960 | tf_op jit(solution)/shard_map/all_gather | solution.py:59
  7.9 0.8 copy-start.4
  7.9 3.6 %copy-start.5 = (bf16[128,6]{0,1:T(8,128)(2,1)S(1)}, bf16[128,6]{0,1:T(8,128)(2,1)}, u32[]{:S(2)}) copy-start(bf16[128,6]{0,1:T(8,128)(2,1)} %param.10) | copy-start | bytes 4612
  7.9 90.4 %all-gather.6.cloned.1.call-start = ((), (), s32[]{:S(2)}) async-start(), calls=%async_computation.5 | async-start | bytes 23592960 | tf_op jit(solution)/shard_map/all_gather | solution.py:58
  12.7 15.4 %all-to-all-start.1 = ((bf16[8,8,14]{2,1,0:T(8,128)(2,1)}), bf16[8,8,14]{2,1,0:T(8,128)(2,1)S(1)}, u32[]{:S(2)}, u32[]{:S(2)}) async-start(bf16[8,8,14]{2,1,0:T(8,128)(2,1)} %convert_element_type.62), calls=%async_computation.1 | async-start | bytes 32768 | tf_op jit(solution)/shard_map/all_to_all | solution.py:55
  28.1 58.0 %all-to-all-start = ((bf16[8,8,14,1280]{3,1,2,0:T(8,128)(2,1)}), bf16[8,8,14,1280]{3,1,2,0:T(8,128)(2,1)S(1)}, u32[]{:S(2)}, u32[]{:S(2)}) async-start(bf16[8,8,14,1280]{3,1,2,0:T(8,128)(2,1)} %copy.55), calls=%async_computation | async-start | bytes 4587520 | tf_op jit(solution)/shard_map/all_to_all | solution.py:54
  34.1 155.5 %all-gather.8.cloned.1.call-start = ((), (), s32[]{:S(2)}) async-start(), calls=%async_computation.6 | async-start | bytes 6266880 | tf_op jit(solution)/shard_map/all_gather | solution.py:95
  180.9 4.4 %copy-start.6 = (s32[128]{0:T(128)S(1)}, s32[128]{0:T(128)}, u32[]{:S(2)}) copy-start(s32[128]{0:T(128)} %param.12) | copy-start | bytes 1540
  183.1 6.5 %copy-start.3 = (bf16[64,1280]{1,0:T(8,128)(2,1)S(1)}, bf16[64,1280]{1,0:T(8,128)(2,1)}, u32[]{:S(2)}) copy-start(bf16[64,1280]{1,0:T(8,128)(2,1)} %param.16) | copy-start | bytes 491524
  185.3 8.9 %copy-start.2 = (bf16[128,1280]{1,0:T(8,128)(2,1)}, bf16[128,1280]{1,0:T(8,128)(2,1)S(1)}, u32[]{:S(2)}) copy-start(bf16[128,1280]{1,0:T(8,128)(2,1)S(1)} %convolution_convert_fusion.2) | copy-start | bytes 983044
  189.7 6.8 %copy-start.1 = (bf16[128,1280]{1,0:T(8,128)(2,1)S(1)}, bf16[128,1280]{1,0:T(8,128)(2,1)}, u32[]{:S(2)}) copy-start(bf16[128,1280]{1,0:T(8,128)(2,1)} %param.9) | copy-start | bytes 983044
Sparse Core Ops, SparseCore 0:
  9.6 30.9 all-gather.3
  42.1 29.8 all-gather.5
  74.3 82.8 all-gather.7
where the time goes:
time: 203 us
  blocking collectives  73.7 us (36%)
  waiting for transfers between devices  53.3 us (26%)
  matrix products  32.8 us (16%)
  between operations  14 us (7%)
  starting transfers between devices  13.4 us (7%)
  local copies, waits for them, and re-layouts  13 us (6%)
  other arithmetic  2.8 us (1%)
    all_to_all x1, blocking collectives, body(): lax.all_to_all(row_grad, 'expert', split_axis=0, concat_axis=0, tiled=True)  69.7 us
    all_to_all x1, waiting for transfers between devices, body(): lax.all_to_all(send_rows, 'expert', split_axis=0, concat_axis=0, tiled=True)  51.2 us
    dot_general x1, matrix products, body(): jnp.einsum('nlcd,lfd->nlcf', recv_rows, full_out, preferred_element_type=...  12.2 us
    dot_general x1, matrix products, body(): jnp.einsum('nlcf,ldf->nlcd', hidden_grad, full_in, preferred_element_type...  11.1 us
    all_to_all x1, starting transfers between devices, body(): lax.all_to_all(gate_slot, 'expert', split_axis=0, concat_axis=0, tiled=True)  7.25 us
    all_to_all x1, starting transfers between devices, body(): lax.all_to_all(send_rows, 'expert', split_axis=0, concat_axis=0, tiled=True)  6 us
    reshape x2, local copies, waits for them, and re-layouts, body(): send_rows.astype(jnp.bfloat16)  5.23 us
    dot_general x1, matrix products, body(): lax.dot_general(adapter_grad, lax.all_gather(w_adapt, ('expert', 'dp'), a...  4.59 us
  transfers between devices with their start and end apart: 5, of which 1 were waited for; matrix products, arithmetic and copies ran while one was open for 21% of the time, Pallas kernels for 0%

commit v1 on v0

--- a/solution.py
+++ b/solution.py
@@ -1,9 +1,12 @@
 import jax
 import jax.numpy as jnp
 from jax import lax
+from jax.experimental import pallas as pl
+from jax.experimental.pallas import tpu as pltpu
 from jax.sharding import PartitionSpec as P
 
 EXPERTS = 64
+TOP = 6
 SIGW = 576
 TILE_R = 8
 
@@ -18,9 +21,8 @@
     return normal_cdf + value * jnp.exp(-0.5 * value * value) * 0.3989422804014327
 
 
-def body(out_grad, gates, routes, tile_slot, w_in, w_out, expert_pre, adapter_pre, w_adapt):
+def row_exchange(out_grad, gates, routes, w_in, w_out, expert_pre):
     axis_count = lax.axis_size("expert")
-    core_count = lax.axis_size("dp")
     tok_count, feature_width = out_grad.shape
     top_count = routes.shape[1]
     local_experts = w_in.shape[0]
@@ -71,9 +73,117 @@
         "nlcf,ldf->nlcd", hidden_grad, full_in, preferred_element_type=jnp.float32
     ).astype(jnp.bfloat16)
     returned = lax.all_to_all(row_grad, "expert", split_axis=0, concat_axis=0, tiled=True)
-    token_grads = jnp.dot(
+    return jnp.dot(
         placing, returned.reshape(slot_total, feature_width), preferred_element_type=jnp.float32
     ).astype(jnp.bfloat16)
+
+
+PAD = 16
+
+
+def expert_kernel(first_ref, rows_in, info, w_out, w_in, pre, out, placed, rows, hidden, back, scale):
+    sources, tokens, _ = rows_in.shape
+    experts = pl.num_programs(0)
+    step = pl.program_id(0)
+    slots = placed.shape[2]
+    depth = pre.shape[2]
+
+    @pl.when(step == 0)
+    def _():
+        first = first_ref[0]
+        slot = lax.broadcasted_iota(jnp.int32, (tokens, slots), 1)
+        expert = (first + slot // PAD).astype(jnp.float32)
+        rank_of = (slot % PAD).astype(jnp.float32)
+        later = lax.broadcasted_iota(jnp.int32, (tokens, tokens), 0)
+        before = (lax.broadcasted_iota(jnp.int32, (tokens, tokens), 1) < later).astype(jnp.bfloat16)
+        for n in range(sources):
+            named = jnp.zeros((tokens, slots), jnp.float32)
+            weight = jnp.zeros((tokens, slots), jnp.float32)
+            table = info[n].astype(jnp.float32)
+            for k in range(TOP):
+                same = (table[:, TOP + k : TOP + k + 1] == expert).astype(jnp.float32)
+                named = named + same
+                weight = weight + same * table[:, k : k + 1]
+            rank = jnp.dot(before, named.astype(jnp.bfloat16), preferred_element_type=jnp.float32)
+            chosen = jnp.where(rank == rank_of, named, 0.0)
+            placed[n] = chosen.astype(jnp.bfloat16)
+            scale[n] = jnp.sum((chosen * weight).T, axis=1, keepdims=True)
+            rows[n] = lax.dot_general(
+                chosen.astype(jnp.bfloat16),
+                rows_in[n],
+                (((0,), (0,)), ((), ())),
+                preferred_element_type=jnp.float32,
+            ).astype(jnp.bfloat16)
+
+    at = pl.ds(pl.multiple_of(step * PAD, PAD), PAD)
+    taken = jnp.concatenate([rows[n, at, :] for n in range(sources)], axis=0)
+    product = lax.dot_general(
+        taken, w_out[0], (((1,), (1,)), ((), ())), preferred_element_type=jnp.float32
+    )
+    for n in range(sources):
+        slope = silu_slope(pre[n, 0].astype(jnp.float32))
+        part = product[n * PAD : n * PAD + depth] * scale[n, pl.ds(step * PAD, depth), :] * slope
+        part = jnp.concatenate([part, jnp.zeros((PAD - depth, part.shape[1]), jnp.float32)], axis=0)
+        hidden[n * PAD : (n + 1) * PAD] = part.astype(jnp.bfloat16)
+    grads = lax.dot_general(
+        hidden[...], w_in[0], (((1,), (1,)), ((), ())), preferred_element_type=jnp.float32
+    ).astype(jnp.bfloat16)
+    for n in range(sources):
+        back[n, at, :] = grads[n * PAD : (n + 1) * PAD]
+
+    @pl.when(step == experts - 1)
+    def _():
+        for n in range(sources):
+            out[n] = jnp.dot(placed[n], back[n], preferred_element_type=jnp.float32).astype(jnp.bfloat16)
+
+
+def block_exchange(out_grad, gates, routes, w_in, w_out, expert_pre):
+    axis_count = lax.axis_size("expert")
+    tok_count, width = out_grad.shape
+    experts, _, fw = w_out.shape[0], w_out.shape[1], w_out.shape[1]
+    depth = expert_pre.shape[2]
+    info = jnp.concatenate([gates, routes.astype(jnp.bfloat16)], axis=1)
+    info = jnp.pad(info, ((0, 0), (0, 128 - 2 * TOP)))
+    info = lax.all_gather(info, "expert", axis=0)
+    rows_in = lax.all_gather(out_grad, "expert", axis=0)
+    full_out = lax.all_gather(w_out, "dp", axis=2, tiled=True)
+    full_in = lax.all_gather(w_in, "dp", axis=1, tiled=True)
+    first = (lax.axis_index("expert") * experts).astype(jnp.int32).reshape(1)
+    slots = experts * PAD
+    whole = lambda *shape: pl.BlockSpec(shape, lambda s: (0,) * len(shape))
+    partial = pl.pallas_call(
+        expert_kernel,
+        grid=(experts,),
+        out_shape=jax.ShapeDtypeStruct((axis_count, tok_count, width), jnp.bfloat16),
+        in_specs=[
+            pl.BlockSpec(memory_space=pltpu.SMEM),
+            whole(axis_count, tok_count, width),
+            whole(axis_count, tok_count, 128),
+            pl.BlockSpec((1, fw, width), lambda s: (s, 0, 0)),
+            pl.BlockSpec((1, width, fw), lambda s: (s, 0, 0)),
+            pl.BlockSpec((axis_count, 1, depth, fw), lambda s: (0, s, 0, 0)),
+        ],
+        out_specs=whole(axis_count, tok_count, width),
+        scratch_shapes=[
+            pltpu.VMEM((axis_count, tok_count, slots), jnp.bfloat16),
+            pltpu.VMEM((axis_count, slots, width), jnp.bfloat16),
+            pltpu.VMEM((axis_count * PAD, fw), jnp.bfloat16),
+            pltpu.VMEM((axis_count, slots, width), jnp.bfloat16),
+            pltpu.VMEM((axis_count, slots, 1), jnp.float32),
+        ],
+        compiler_params=pltpu.CompilerParams(vmem_limit_bytes=50 << 20),
+    )(first, rows_in, info, full_out, full_in, expert_pre)
+    return lax.psum_scatter(partial.reshape(axis_count * tok_count, width), "expert", scatter_dimension=0, tiled=True)
+
+
+def body(out_grad, gates, routes, tile_slot, w_in, w_out, expert_pre, adapter_pre, w_adapt):
+    core_count = lax.axis_size("dp")
+    feature_width = out_grad.shape[1]
+    if lax.axis_size("expert") <= 8 and out_grad.shape[0] % 128 == 0 and expert_pre.shape[2] <= PAD:
+        exchange = block_exchange
+    else:
+        exchange = row_exchange
+    token_grads = exchange(out_grad, gates, routes, w_in, w_out, expert_pre)
     vis_count = adapter_pre.shape[0]
     owner_hot = (
         tile_slot[None, :] == jnp.arange(core_count * vis_count, dtype=jnp.int32)[:, None]

time: 203 us -> 269 us (1.33)
  waiting for transfers between devices: 53.3 us -> 188 us
  blocking collectives: 73.7 us -> 33.3 us
  matrix products: 32.8 us -> 5.74 us
  Pallas kernels: 0 us -> 22.2 us
  starting transfers between devices: 13.4 us -> 0.2 us
  local copies, waits for them, and re-layouts: 13 us -> 3.18 us
  other arithmetic: 2.8 us -> 0.06 us
    reduce_scatter x0 -> x1, waiting for transfers between devices: none -> 95.9 us  [block_exchange(): lax.psum_scatter(partial.reshape(axis_count * tok_count, width), 'expert'...]
    all_gather x2 -> x3, waiting for transfers between devices: 0.01 us -> 89.8 us  [the longest x1 31.4 us: block_exchange(): full_in = lax.all_gather(w_in, 'dp', axis=1, tiled=True)]
    all_to_all x1 -> x0, blocking collectives: 69.7 us -> none  [body(): lax.all_to_all(row_grad, 'expert', split_axis=0, concat_axis=0, tiled=True)]
    all_to_all x2 -> x0, waiting for transfers between devices: 51.2 us -> none  [the longest x1 51.2 us: body(): lax.all_to_all(send_rows, 'expert', split_axis=0, concat_axis=0, tiled=True)]
    all_gather x0 -> x1, blocking collectives: none -> 29.3 us  [block_exchange(): info = lax.all_gather(info, 'expert', axis=0)]
    dot_general x4 -> x0, matrix products: 28 us -> none  [the longest x1 12.2 us: body(): jnp.einsum('nlcd,lfd->nlcf', recv_rows, full_out, preferred_element_type=...]
    pallas_call x0 -> x1, Pallas kernels: none -> 22.2 us  [block_exchange(): pl.pallas_call(expert_kernel, grid=(experts,), out_shape=jax.ShapeDtypeSt...]
    all_to_all x2 -> x0, starting transfers between devices: 13.2 us -> none  [the longest x1 7.25 us: body(): lax.all_to_all(gate_slot, 'expert', split_axis=0, concat_axis=0, tiled=True)]
  transfers between devices with their start and end apart: 5 -> 5, of which waited for: 1 -> 4; matrix products, arithmetic and copies ran while one was open for 21% -> 1% of each run, Pallas kernels for 0% -> 0%
where the time goes in v1:
time: 269 us; the launch traced here: 268 us
  waiting for transfers between devices  188 us (70%)
  blocking collectives  33.3 us (12%)
  Pallas kernels  22.2 us (8%)
  between operations  15.3 us (6%)
  matrix products  5.74 us (2%)
  local copies, waits for them, and re-layouts  3.18 us (1%)
    reduce_scatter x1, waiting for transfers between devices, block_exchange(): lax.psum_scatter(partial.reshape(axis_count * tok_count, width), 'expert'...  95.9 us
    all_gather x1, waiting for transfers between devices, block_exchange(): full_in = lax.all_gather(w_in, 'dp', axis=1, tiled=True)  31.4 us
    all_gather x1, waiting for transfers between devices, block_exchange(): rows_in = lax.all_gather(out_grad, 'expert', axis=0)  29.9 us
    all_gather x1, blocking collectives, block_exchange(): info = lax.all_gather(info, 'expert', axis=0)  29.3 us
    all_gather x1, waiting for transfers between devices, block_exchange(): full_out = lax.all_gather(w_out, 'dp', axis=2, tiled=True)  28.4 us
    pallas_call x1, Pallas kernels, block_exchange(): pl.pallas_call(expert_kernel, grid=(experts,), out_shape=jax.ShapeDtypeSt...  22.2 us
  transfers between devices with their start and end apart: 5, of which 4 were waited for; matrix products, arithmetic and copies ran while one was open for 1% of the time, Pallas kernels for 0%

profile of v1, /device:TPU:0, one launch (start us, length us, event | category | flops | bytes accessed | tf_op | source)
XLA Modules:
  0.0 268.3 jit_solution(17989715246873789557)
XLA Ops:
  8.0 0.0 all-gather.13.cloned.1.call-start
  8.0 0.7 all-gather.13.cloned.1.call-update
  8.7 0.0 all-gather.7.cloned.1.call-start
  8.8 0.7 all-gather.7.cloned.1.call-update
  9.5 0.0 copy-start
  9.5 0.0 copy-start.2
  9.5 0.0 copy-start.3
  9.5 0.0 all-gather.9.cloned.1.call-start
  9.6 0.7 all-gather.9.cloned.1.call-update
  10.2 0.0 reduce-scatter.2.cloned.1.call-start
  10.3 0.5 copy-done
  10.8 0.3 copy.12.pre
  11.1 0.0 copy-done.2
  11.2 0.0 copy-done.3
  11.2 29.3 %all-gather.1 = bf16[1024,128]{0,1:T(8,128)(2,1)S(1)} all-gather(bf16[128,128]{0,1:T(8,128)(2,1)S(1)} %fusion.17), channel_id=3, replica_groups=mesh['groups'=2,'expert'=8,'dp'=2] {'expert'}, dimensions={0}, use_global_device_ids=true | all-gather | bytes 294912 | tf_op jit(solution)/shard_map/all_gather | solution.py:147
  40.5 0.2 copy.11
  40.6 29.9 %all-gather.13.cloned.1.call-done = bf16[1024,1280]{1,0:T(8,128)(2,1)} async-done(((bf16[128,1280]{1,0:T(8,128)(2,1)}), bf16[1024,1280]{1,0:T(8,128)(2,1)}) %all-gather.13.cloned.1.call-update) | async-done | bytes 2621456 | tf_op jit(solution)/shard_map/all_gather | solution.py:148
  70.6 28.4 %all-gather.7.cloned.1.call-done.w_out = bf16[8,768,1280]{2,1,0:T(8,128)(2,1)} async-done(((bf16[8,768,640]{2,1,0:T(8,128)(2,1)}), bf16[8,768,1280]{2,1,0:T(8,128)(2,1)}) %all-gather.7.cloned.1.call-update) | async-done | bytes 15728656 | tf_op jit(solution)/shard_map/all_gather | solution.py:149
  99.0 31.4 %all-gather.9.cloned.1.call-done.w_in = bf16[8,1280,768]{2,1,0:T(8,128)(2,1)} async-done(((bf16[8,640,768]{2,1,0:T(8,128)(2,1)}), bf16[8,1280,768]{2,1,0:T(8,128)(2,1)}) %all-gather.9.cloned.1.call-update) | async-done | bytes 15728656 | tf_op jit(solution)/shard_map/all_gather | solution.py:150
  130.4 0.0 copy-start.4
  130.4 0.0 copy-start.1
  130.4 22.2 %shard_map.104 = bf16[8,128,1280]{2,1,0:T(8,128)(2,1)} custom-call(s32[1]{0:T(128)} %bitcast.first_ref, bf16[8,128,1280]{2,1,0:T(8,128)(2,1)} %bitcast.10, bf16[8,128,128]{2,1,0:T(8,128)(2,1)S(1)} %bitcast.8, bf16[8,768,1280]{2,1,0:T(8,128)(2,1)} %all-gather.7.cloned.1.call-done.w_out, bf16[8,1280,768]{2,1,0:T(8,128)(2,1)} %all-gather.9.cloned.1.call-done.w_in, ...), custom_call_target="tpu_custom_call" | custom-call | tf_op jit(solution)/shard_map/pallas_call | solution.py:154
  152.6 0.0 reduce-scatter.2.cloned.1.call-update
  152.6 0.0 all-gather.11.cloned.1.call-start
  152.7 0.5 all-gather.11.cloned.1.call-update
  153.2 95.9 %reduce-scatter.2.cloned.1.call-done = bf16[128,1280]{1,0:T(8,128)(2,1)} async-done(((bf16[1024,1280]{1,0:T(8,128)(2,1)}), bf16[128,1280]{1,0:T(8,128)(2,1)}) %reduce-scatter.2.cloned.1.call-update) | async-done | bytes 327696 | tf_op jit(solution)/shard_map/reduce_scatter | solution.py:176
  249.1 0.0 copy-done.4
  249.1 1.2 convolution_convert_fusion
  250.3 4.0 %all_to_all.5 = bf16[2,64,1280]{2,1,0:T(8,128)(2,1)S(1)} all-to-all(bf16[2,64,1280]{2,1,0:T(8,128)(2,1)S(1)} %bitcast.12), channel_id=1, replica_groups=mesh['groups'=2,'expert'=8,'dp'=2] {'dp'}, dimensions={0} | all-to-all | bytes 655360 | tf_op jit(solution)/shard_map/all_to_all | solution.py:194
  254.4 0.0 all-gather.11.cloned.1.call-done
  254.4 0.0 copy-done.1
  254.4 4.5 %fusion.8 = f32[64,2304]{1,0:T(8,128)S(1)} fusion(bf16[2304,1280]{1,0:T(8,128)(2,1)} %all-gather.11.cloned.1.call-done, f32[64,1280]{1,0:T(8,128)S(1)} %convert_reduce_fusion, bf16[64,1280]{1,0:T(8,128)(2,1)S(1)} %copy-done.1), kind=kOutput, calls=%fused_computation.14 | convolution fusion | flops 378388480 | bytes 6979584 | tf_op jit(solution)/shard_map/dot_general | solution.py:203
  259.0 0.5 reshape.23
  259.5 0.1 copy.13
  259.6 1.5 reshape.24
  (3 shorter events, 0.1 us)
Async XLA Ops:
  8.0 62.6 %all-gather.13.cloned.1.call-start = ((), (), s32[]{:S(2)}) async-start(), calls=%async_computation.6 | async-start | bytes 2949120 | tf_op jit(solution)/shard_map/all_gather | solution.py:148
  8.7 90.2 %all-gather.7.cloned.1.call-start = ((), (), s32[]{:S(2)}) async-start(), calls=%async_computation.2 | async-start | bytes 23592960 | tf_op jit(solution)/shard_map/all_gather | solution.py:149
  9.5 1.3 copy-start
  9.5 1.6 copy-start.2
  9.5 1.7 copy-start.3
  9.5 120.9 %all-gather.9.cloned.1.call-start = ((), (), s32[]{:S(2)}) async-start(), calls=%async_computation.3 | async-start | bytes 23592960 | tf_op jit(solution)/shard_map/all_gather | solution.py:150
  10.2 238.9 %reduce-scatter.2.cloned.1.call-start = ((), (), s32[]{:S(2)}) async-start(), calls=%async_computation.4 | async-start | bytes 2949120 | tf_op jit(solution)/shard_map/reduce_scatter | solution.py:176
  130.4 118.7 %copy-start.4 = (s32[128]{0:T(128)S(1)}, s32[128]{0:T(128)}, u32[]{:S(2)}) copy-start(s32[128]{0:T(128)} %param.12) | copy-start | bytes 1540
  130.4 124.0 %copy-start.1 = (bf16[64,1280]{1,0:T(8,128)(2,1)S(1)}, bf16[64,1280]{1,0:T(8,128)(2,1)}, u32[]{:S(2)}) copy-start(bf16[64,1280]{1,0:T(8,128)(2,1)} %param.16) | copy-start | bytes 491524
  152.6 101.8 %all-gather.11.cloned.1.call-start = ((), (), s32[]{:S(2)}) async-start(), calls=%async_computation.5 | async-start | bytes 6266880 | tf_op jit(solution)/shard_map/all_gather | solution.py:205
Sparse Core Ops, SparseCore 0:
  11.0 59.4 all-gather.12
  72.1 26.8 all-gather.6
  100.5 29.8 all-gather.8
  152.8 96.3 reduce-scatter.1
Sparse Core Ops, SparseCore 1:
  155.4 68.6 all-gather.10

commit v2 on v0

--- a/solution.py
+++ b/solution.py
@@ -1,9 +1,12 @@
 import jax
 import jax.numpy as jnp
 from jax import lax
+from jax.experimental import pallas as pl
+from jax.experimental.pallas import tpu as pltpu
 from jax.sharding import PartitionSpec as P
 
 EXPERTS = 64
+TOP = 6
 SIGW = 576
 TILE_R = 8
 
@@ -18,7 +21,7 @@
     return normal_cdf + value * jnp.exp(-0.5 * value * value) * 0.3989422804014327
 
 
-def body(out_grad, gates, routes, tile_slot, w_in, w_out, expert_pre, adapter_pre, w_adapt):
+def row_exchange(out_grad, gates, routes, tile_slot, w_in, w_out, expert_pre, vis_count):
     axis_count = lax.axis_size("expert")
     core_count = lax.axis_size("dp")
     tok_count, feature_width = out_grad.shape
@@ -74,7 +77,6 @@
     token_grads = jnp.dot(
         placing, returned.reshape(slot_total, feature_width), preferred_element_type=jnp.float32
     ).astype(jnp.bfloat16)
-    vis_count = adapter_pre.shape[0]
     owner_hot = (
         tile_slot[None, :] == jnp.arange(core_count * vis_count, dtype=jnp.int32)[:, None]
     ).astype(jnp.bfloat16)
@@ -88,7 +90,270 @@
         concat_axis=0,
         tiled=True,
     )
-    visual_grad = jnp.sum(incoming.astype(jnp.float32), axis=0)
+    return token_grads, jnp.sum(incoming.astype(jnp.float32), axis=0)
+
+
+PAD = 16
+MESH = pl.DeviceIdType.MESH
+
+
+def seat_of(index, count):
+    odd, half = index % 2, index // 2
+    return half * (1 - odd) + (count - 1 - half) * odd
+
+
+def index_of(seat, count):
+    back = seat // (count // 2)
+    return 2 * seat * (1 - back) + (2 * (count - 1 - seat) + 1) * back
+
+
+def exchange_kernel(
+    x, info, slot_row, pre, w_out, w_in, token_out, visual_out,
+    xs, infos, wo, wi, placed, rows, back, scale, hidden, outbox, inbox, vis_send, vis_recv,
+    x_send, x_recv, i_send, i_recv, w_local, w_send, w_recv, r_send, r_recv, v_send, v_recv,
+):
+    count, tokens, width = xs.shape
+    experts, fw, half_width = wo.shape[1], wo.shape[2], wo.shape[3]
+    slots = experts * PAD
+    depth = pre.shape[2]
+    half = tokens // 2
+    far = count // 2
+    core = lax.axis_index("dp")
+    expert_index = lax.axis_index("expert")
+    seat = seat_of(expert_index, count)
+    right = {"expert": index_of((seat + 1) % count, count)}
+    left = {"expert": index_of((seat + count - 1) % count, count)}
+    sibling = {"dp": 1 - core}
+
+    def own_weight(l, which):
+        source, target = ((w_out, wo), (w_in, wi))[which]
+        return pltpu.make_async_copy(source.at[l], target.at[core, l], w_local.at[which, l])
+
+    def sent_weight(l, which):
+        source, target = ((w_out, wo), (w_in, wi))[which]
+        return pltpu.make_async_remote_copy(
+            source.at[l], target.at[core, l], w_send.at[which, l], w_recv.at[which, l],
+            device_id=sibling, device_id_type=MESH,
+        )
+
+    barrier = pltpu.get_barrier_semaphore()
+    for other in (left, right, sibling):
+        pl.semaphore_signal(barrier, inc=1, device_id=other, device_id_type=MESH)
+    pl.semaphore_wait(barrier, 3)
+
+    def ring(step, way):
+        come, go = (step - 1, step) if way == 0 else ((count - step + 1) % count, count - step)
+        block = x if step == 1 else xs.at[come]
+        note = info if step == 1 else infos.at[come]
+        to = (right, left)[way]
+        copies = []
+        at = pl.ds(way * half, half) if step == far else pl.ds(0, tokens)
+        copies.append(
+            pltpu.make_async_remote_copy(
+                block.at[at], xs.at[go, at], x_send.at[way, step], x_recv.at[way, step],
+                device_id=to, device_id_type=MESH,
+            )
+        )
+        if step < far or way == 0:
+            copies.append(
+                pltpu.make_async_remote_copy(
+                    note, infos.at[go], i_send.at[way, step], i_recv.at[way, step],
+                    device_id=to, device_id_type=MESH,
+                )
+            )
+        return copies
+
+    sends = [ring(1, 0), ring(1, 1)]
+    for copies in sends:
+        for copy in copies:
+            copy.start()
+
+    @pl.loop(0, experts)
+    def _(l):
+        for which in range(2):
+            sent_weight(l, which).start()
+            own_weight(l, which).start()
+
+    slot = lax.broadcasted_iota(jnp.int32, (slots, tokens), 0)
+    expert = (expert_index * experts + slot // PAD).astype(jnp.float32)
+    rank_of = (slot % PAD).astype(jnp.float32)
+    before = (
+        lax.broadcasted_iota(jnp.int32, (tokens, tokens), 0)
+        < lax.broadcasted_iota(jnp.int32, (tokens, tokens), 1)
+    ).astype(jnp.bfloat16)
+
+    def take(offset):
+        block = x if offset == 0 else xs.at[offset]
+        table = (info if offset == 0 else infos.at[offset])[...].astype(jnp.float32)
+        named = jnp.zeros((slots, tokens), jnp.float32)
+        weight = jnp.zeros((slots, tokens), jnp.float32)
+        for k in range(TOP):
+            same = (table[TOP + k : TOP + k + 1, :] == expert).astype(jnp.float32)
+            named = named + same
+            weight = weight + same * table[k : k + 1, :]
+        rank = jnp.dot(named.astype(jnp.bfloat16), before, preferred_element_type=jnp.float32)
+        chosen = jnp.where(rank == rank_of, named, 0.0)
+        placed[offset] = chosen.astype(jnp.bfloat16)
+        scale[offset] = jnp.sum(chosen * weight, axis=1, keepdims=True)
+        rows[offset] = jnp.dot(
+            chosen.astype(jnp.bfloat16), block[...], preferred_element_type=jnp.float32
+        ).astype(jnp.bfloat16)
+
+    take(0)
+    for step in range(1, far + 1):
+        for copies in sends:
+            for copy in copies:
+                copy.wait()
+        if step < far:
+            sends = [ring(step + 1, 0), ring(step + 1, 1)]
+            for copies in sends:
+                for copy in copies:
+                    copy.start()
+        take(step)
+        if step < far:
+            take(count - step)
+
+    @pl.loop(0, experts)
+    def _(l):
+        for which in range(2):
+            own_weight(l, which).wait()
+            sent_weight(l, which).wait()
+        at = pl.ds(pl.multiple_of(l * PAD, PAD), PAD)
+        taken = jnp.concatenate([rows[o, at, :] for o in range(count)], axis=0)
+        product = lax.dot_general(
+            taken[:, :half_width], wo[0, l], (((1,), (1,)), ((), ())), preferred_element_type=jnp.float32
+        ) + lax.dot_general(
+            taken[:, half_width:], wo[1, l], (((1,), (1,)), ((), ())), preferred_element_type=jnp.float32
+        )
+        for o in range(count):
+            source = index_of((seat + count - o) % count, count)
+            slope = silu_slope(pre[source, l].astype(jnp.float32))
+            part = product[o * PAD : o * PAD + depth] * scale[o, at, :][:depth] * slope
+            part = jnp.concatenate([part, jnp.zeros((PAD - depth, fw), jnp.float32)], axis=0)
+            hidden[o * PAD : (o + 1) * PAD] = part.astype(jnp.bfloat16)
+        for c in range(2):
+            grads = lax.dot_general(
+                hidden[...], wi[c, l], (((1,), (1,)), ((), ())), preferred_element_type=jnp.float32
+            ).astype(jnp.bfloat16)
+            for o in range(count):
+                back[o, at, c * half_width : (c + 1) * half_width] = grads[o * PAD : (o + 1) * PAD]
+
+    def total(offset):
+        return lax.dot_general(
+            placed[offset], back[offset], (((0,), (0,)), ((), ())), preferred_element_type=jnp.float32
+        )
+
+    def hop(step, way):
+        at = pl.ds(way * half, half) if step == 1 else pl.ds(0, tokens)
+        return pltpu.make_async_remote_copy(
+            outbox.at[way, step - 1, at], inbox.at[way, step - 1, at],
+            r_send.at[way, step - 1], r_recv.at[way, step - 1],
+            device_id=(right, left)[way], device_id_type=MESH,
+        )
+
+    outbox[0, 0] = total(far).astype(jnp.bfloat16)
+    outbox[1, 0, half:] = outbox[0, 0, half:]
+    hops = [hop(1, 0), hop(1, 1)]
+    for copy in hops:
+        copy.start()
+    for step in range(2, far + 1):
+        distance = far + 1 - step
+        mine = [total(count - distance), total(distance)]
+        later = []
+        for way in range(2):
+            hops[way].wait()
+            if step == 2:
+                at = slice(way * half, (way + 1) * half)
+                rest = slice((1 - way) * half, (2 - way) * half)
+                outbox[way, 1, at] = (
+                    mine[way][at] + inbox[way, 0, at].astype(jnp.float32)
+                ).astype(jnp.bfloat16)
+                outbox[way, 1, rest] = mine[way][rest].astype(jnp.bfloat16)
+            else:
+                outbox[way, step - 1] = (
+                    mine[way] + inbox[way, step - 2].astype(jnp.float32)
+                ).astype(jnp.bfloat16)
+            copy = hop(step, way)
+            copy.start()
+            later.append(copy)
+        hops = later
+    result = total(0)
+    for way in range(2):
+        hops[way].wait()
+        result = result + inbox[way, far - 1].astype(jnp.float32)
+    result = result.astype(jnp.bfloat16)
+    token_out[...] = result
+
+    vis = visual_out.shape[0]
+    row = lax.broadcasted_iota(jnp.int32, (vis, tokens), 0)
+    theirs = (slot_row[...] == row + (1 - core) * vis).astype(jnp.bfloat16)
+    vis_send[...] = jnp.dot(theirs, result, preferred_element_type=jnp.float32).astype(jnp.bfloat16)
+    copy = pltpu.make_async_remote_copy(
+        vis_send, vis_recv, v_send, v_recv, device_id=sibling, device_id_type=MESH
+    )
+    copy.start()
+    ours = (slot_row[...] == row + core * vis).astype(jnp.bfloat16)
+    kept = jnp.dot(ours, result, preferred_element_type=jnp.float32)
+    copy.wait()
+    visual_out[...] = (kept + vis_recv[...].astype(jnp.float32)).astype(jnp.bfloat16)
+
+
+def block_exchange(out_grad, gates, routes, tile_slot, w_in, w_out, expert_pre, vis_count):
+    count = lax.axis_size("expert")
+    tokens, width = out_grad.shape
+    experts, fw, half_width = w_out.shape
+    info = jnp.concatenate([gates.T, routes.T.astype(jnp.bfloat16)], axis=0)
+    info = jnp.pad(info, ((0, PAD - 2 * TOP), (0, 0)))
+    slots = experts * PAD
+    bf16 = jnp.bfloat16
+    dma = pltpu.SemaphoreType.DMA
+    far = count // 2
+    vmem = pl.BlockSpec(memory_space=pltpu.VMEM)
+    token_grads, visual = pl.pallas_call(
+        exchange_kernel,
+        out_shape=(
+            jax.ShapeDtypeStruct((tokens, width), bf16),
+            jax.ShapeDtypeStruct((vis_count, width), bf16),
+        ),
+        in_specs=[vmem] * 4 + [pl.BlockSpec(memory_space=pl.ANY)] * 2,
+        out_specs=(vmem, vmem),
+        scratch_shapes=[
+            pltpu.VMEM((count, tokens, width), bf16),
+            pltpu.VMEM((count, PAD, tokens), bf16),
+            pltpu.VMEM((2, experts, fw, half_width), bf16),
+            pltpu.VMEM((2, experts, half_width, fw), bf16),
+            pltpu.VMEM((count, slots, tokens), bf16),
+            pltpu.VMEM((count, slots, width), bf16),
+            pltpu.VMEM((count, slots, width), bf16),
+            pltpu.VMEM((count, slots, 1), jnp.float32),
+            pltpu.VMEM((count * PAD, fw), bf16),
+            pltpu.VMEM((2, far, tokens, width), bf16),
+            pltpu.VMEM((2, far, tokens, width), bf16),
+            pltpu.VMEM((vis_count, width), bf16),
+            pltpu.VMEM((vis_count, width), bf16),
+            dma((2, far + 1)), dma((2, far + 1)), dma((2, far + 1)), dma((2, far + 1)),
+            dma((2, experts)), dma((2, experts)), dma((2, experts)),
+            dma((2, far)), dma((2, far)), dma, dma,
+        ],
+        compiler_params=pltpu.CompilerParams(
+            collective_id=0, has_side_effects=True, vmem_limit_bytes=58 << 20
+        ),
+        cost_estimate=pl.CostEstimate(
+            flops=4 * experts * count * PAD * width * fw, bytes_accessed=4 * experts * width * fw, transcendentals=0
+        ),
+    )(out_grad, info, tile_slot.reshape(1, tokens), expert_pre, w_out, w_in)
+    return token_grads, visual.astype(jnp.float32)
+
+
+def body(out_grad, gates, routes, tile_slot, w_in, w_out, expert_pre, adapter_pre, w_adapt):
+    vis_count = adapter_pre.shape[0]
+    if lax.axis_size("expert") == 8 and out_grad.shape[0] == 128 and expert_pre.shape[2] <= PAD:
+        exchange = block_exchange
+    else:
+        exchange = row_exchange
+    token_grads, visual_grad = exchange(
+        out_grad, gates, routes, tile_slot, w_in, w_out, expert_pre, vis_count
+    )
     adapter_grad = (visual_grad * gelu_slope(adapter_pre.astype(jnp.float32))).astype(jnp.bfloat16)
     shuffled = lax.dot_general(
         adapter_grad,

time: 203 us -> 138 us (0.68)
  Pallas kernels: 0 us -> 110 us
  blocking collectives: 73.7 us -> 0 us
  waiting for transfers between devices: 53.3 us -> 0.7 us
  matrix products: 32.8 us -> 4.69 us
  starting transfers between devices: 13.4 us -> 0.04 us
  local copies, waits for them, and re-layouts: 13 us -> 5.7 us
    pallas_call x0 -> x1, Pallas kernels: none -> 110 us  [block_exchange(): pl.pallas_call(exchange_kernel, out_shape=(jax.ShapeDtypeStruct((tokens,...]
    all_to_all x2 -> x0, blocking collectives: 73.7 us -> none  [the longest x1 69.7 us: body(): lax.all_to_all(row_grad, 'expert', split_axis=0, concat_axis=0, tiled=True)]
    all_to_all x2 -> x0, waiting for transfers between devices: 51.2 us -> none  [the longest x1 51.2 us: body(): lax.all_to_all(send_rows, 'expert', split_axis=0, concat_axis=0, tiled=True)]
    dot_general x5 -> x0, matrix products: 28.2 us -> none  [the longest x1 12.2 us: body(): jnp.einsum('nlcd,lfd->nlcf', recv_rows, full_out, preferred_element_type=...]
    all_to_all x2 -> x0, starting transfers between devices: 13.2 us -> none  [the longest x1 7.25 us: body(): lax.all_to_all(gate_slot, 'expert', split_axis=0, concat_axis=0, tiled=True)]
    reshape x3 -> x0, local copies, waits for them, and re-layouts: 7.43 us -> none  [the longest x2 5.23 us: body(): send_rows.astype(jnp.bfloat16)]
    unnamed x15 -> x6, local copies, waits for them, and re-layouts: 0.17 us -> 3.54 us
  transfers between devices with their start and end apart: 5 -> 1, of which waited for: 1 -> 0; matrix products, arithmetic and copies ran while one was open for 21% -> 3% of each run, Pallas kernels for 0% -> 80%
where the time goes in v2:
time: 138 us
  Pallas kernels  110 us (80%)
  between operations  14.1 us (10%)
  local copies, waits for them, and re-layouts  5.7 us (4%)
  matrix products  4.69 us (3%)
  other arithmetic  1.97 us (1%)
    pallas_call x1, Pallas kernels, block_exchange(): pl.pallas_call(exchange_kernel, out_shape=(jax.ShapeDtypeStruct((tokens,...  110 us
    dot_general x1, matrix products, body(): lax.dot_general(adapter_grad, lax.all_gather(w_adapt, ('expert', 'dp'), a...  4.69 us
    unnamed x6, local copies, waits for them, and re-layouts  3.54 us
  transfers between devices with their start and end apart: 1, of which 0 were waited for; matrix products, arithmetic and copies ran while one was open for 3% of the time, Pallas kernels for 80%

profile of v2, /device:TPU:0, one launch (start us, length us, event | category | flops | bytes accessed | tf_op | source)
XLA Modules:
  0.0 137.5 jit_solution(16447847728026478957)
XLA Ops:
  7.2 0.0 all-gather.2.cloned.1.call-start
  7.2 0.7 all-gather.2.cloned.1.call-update
  7.9 2.8 %copy.11.pre = bf16[8,8,14,768]{3,2,1,0:T(8,128)(2,1)} copy(bf16[8,8,14,768]{3,1,2,0:T(8,128)(2,1)} %param.15) | data formatting | bytes 2752512 | tf_op args[6]
  10.7 0.7 convert_bitcast_fusion
  11.4 1.3 fusion.17.info
  12.7 0.0 copy-start.1
  12.7 110.3 %shard_map.104 = (bf16[128,1280]{1,0:T(8,128)(2,1)}, bf16[64,1280]{1,0:T(8,128)(2,1)}) custom-call(bf16[128,1280]{1,0:T(8,128)(2,1)} %x.3, bf16[16,128]{1,0:T(8,128)(2,1)} %fusion.17.info, s32[1,128]{1,0:T(1,128)} %bitcast.8, bf16[8,8,14,768]{3,2,1,0:T(8,128)(2,1)} %copy.11.pre, bf16[8,768,640]{2,1,0:T(8,128)(2,1)} %w_out.1, bf16[8,640,768]{2,1,0:T(8,128)(2,1)} %w_in.1), custom_call_target="tpu_custom_call" | custom-call | flops 4026531840 | bytes 31457280 | tf_op jit(solution)/shard_map/pallas_call | solution.py:312
  123.0 0.0 copy-start
  123.0 0.0 all-gather.2.cloned.1.call-done
  123.1 0.0 copy-done.1
  123.1 4.7 %fusion.8 = f32[64,2304]{1,0:T(8,128)S(1)} fusion(bf16[2304,1280]{1,0:T(8,128)(2,1)} %all-gather.2.cloned.1.call-done, bf16[64,1280]{1,0:T(8,128)(2,1)S(1)} %copy-done.1, bf16[64,1280]{1,0:T(8,128)(2,1)} %get-tuple-element.5), kind=kOutput, calls=%fused_computation.12 | convolution fusion | flops 378470400 | bytes 6815744 | tf_op jit(solution)/shard_map/dot_general | solution.py:358
  127.8 0.5 reshape.14
  128.3 0.1 copy.12
  128.4 1.5 %reshape.15 = f32[16,9216]{1,0:T(8,128)} reshape(f32[8,2,8,2,576]{4,3,2,1,0:T(2,128)S(1)} %copy.12) | data formatting | bytes 1179648 | tf_op jit(solution)/shard_map/reshape | solution.py:366
  129.9 0.0 copy-done
  129.9 0.7 copy.14
Async XLA Ops:
  7.2 115.9 %all-gather.2.cloned.1.call-start = ((), (), s32[]{:S(2)}) async-start(), calls=%async_computation | async-start | bytes 6266880 | tf_op jit(solution)/shard_map/all_gather | solution.py:360
  12.7 110.4 %copy-start.1 = (bf16[64,1280]{1,0:T(8,128)(2,1)S(1)}, bf16[64,1280]{1,0:T(8,128)(2,1)}, u32[]{:S(2)}) copy-start(bf16[64,1280]{1,0:T(8,128)(2,1)} %param.16) | copy-start | bytes 491524
  123.0 6.9 %copy-start = (bf16[128,1280]{1,0:T(8,128)(2,1)S(1)}, bf16[128,1280]{1,0:T(8,128)(2,1)}, u32[]{:S(2)}) copy-start(bf16[128,1280]{1,0:T(8,128)(2,1)} %get-tuple-element.8) | copy-start | bytes 983044
Sparse Core Ops, SparseCore 0:
  10.3 72.7 all-gather.1

commit v3 on v2

--- a/solution.py
+++ b/solution.py
@@ -108,9 +108,10 @@
 
 
 def exchange_kernel(
-    x, info, slot_row, pre, w_out, w_in, token_out, visual_out,
-    xs, infos, wo, wi, placed, rows, back, scale, hidden, outbox, inbox, vis_send, vis_recv,
+    x, info, slot_row, pre, slope_in, w_out, w_in, w_adapt, token_out, shuffled_out,
+    xs, infos, wo, wi, placed, rows, back, scale, hidden, outbox, inbox, vis_send, vis_recv, wa,
     x_send, x_recv, i_send, i_recv, w_local, w_send, w_recv, r_send, r_recv, v_send, v_recv,
+    a_own, a_send, a_recv, y_send, y_recv, s_send, s_recv,
 ):
     count, tokens, width = xs.shape
     experts, fw, half_width = wo.shape[1], wo.shape[2], wo.shape[3]
@@ -124,6 +125,45 @@
     right = {"expert": index_of((seat + 1) % count, count)}
     left = {"expert": index_of((seat + count - 1) % count, count)}
     sibling = {"dp": 1 - core}
+    group = lax.axis_index("groups")
+    twin = {"groups": 1 - group}
+    shard = w_adapt.shape[0]
+    cut = (shard // 2 + PAD - 1) // PAD * PAD
+
+    def columns(which):
+        return pl.ds(pl.multiple_of(which * half_width, 128), half_width)
+
+    def shard_at(offset, start=0, size=None):
+        owner = index_of((seat + count - offset) % count, count)
+        first = pl.multiple_of((owner * 2 + core) * shard + start, PAD)
+        return pl.ds(first, shard if size is None else size)
+
+    def adapt_ring(step, way):
+        offset = step - 1 if way == 0 else (count - step + 1) % count
+        start, size = (0, shard) if step < far else ((0, cut), (cut, shard - cut))[way]
+        place = wa.at[shard_at(offset, start, size), columns(group)]
+        source = w_adapt.at[pl.ds(start, size), columns(group)] if step == 1 else place
+        return pltpu.make_async_remote_copy(
+            source, place, a_send.at[way, step], a_recv.at[way, step],
+            device_id=(right, left)[way], device_id_type=MESH,
+        )
+
+    def adapt_twin(offset):
+        place = wa.at[shard_at(offset), columns(group)]
+        return pltpu.make_async_remote_copy(
+            place, place, y_send.at[offset], y_recv.at[offset], device_id=twin, device_id_type=MESH
+        )
+
+    def adapt_sibling(offset, mine):
+        which = group if mine == 0 else 1 - group
+        place = wa.at[shard_at(offset), columns(which)]
+        source = w_adapt.at[:, columns(which)] if offset == 0 else place
+        return pltpu.make_async_remote_copy(
+            source, place, s_send.at[mine, offset], s_recv.at[mine, offset],
+            device_id=sibling, device_id_type=MESH,
+        )
+
+    adapt_own = pltpu.make_async_copy(w_adapt, wa.at[shard_at(0)], a_own)
 
     def own_weight(l, which):
         source, target = ((w_out, wo), (w_in, wi))[which]
@@ -137,9 +177,9 @@
         )
 
     barrier = pltpu.get_barrier_semaphore()
-    for other in (left, right, sibling):
+    for other in (left, right, sibling, twin):
         pl.semaphore_signal(barrier, inc=1, device_id=other, device_id_type=MESH)
-    pl.semaphore_wait(barrier, 3)
+    pl.semaphore_wait(barrier, 4)
 
     def ring(step, way):
         come, go = (step - 1, step) if way == 0 else ((count - step + 1) % count, count - step)
@@ -173,6 +213,10 @@
         for which in range(2):
             sent_weight(l, which).start()
             own_weight(l, which).start()
+
+    adapt_own.start()
+    for mine in range(2):
+        adapt_sibling(0, mine).start()
 
     slot = lax.broadcasted_iota(jnp.int32, (slots, tokens), 0)
     expert = (expert_index * experts + slot // PAD).astype(jnp.float32)
@@ -209,12 +253,14 @@
             for copies in sends:
                 for copy in copies:
                     copy.start()
+        else:
+            for way in range(2):
+                adapt_ring(1, way).start()
         take(step)
         if step < far:
             take(count - step)
 
-    @pl.loop(0, experts)
-    def _(l):
+    def one_expert(l):
         for which in range(2):
             own_weight(l, which).wait()
             sent_weight(l, which).wait()
@@ -237,6 +283,18 @@
             ).astype(jnp.bfloat16)
             for o in range(count):
                 back[o, at, c * half_width : (c + 1) * half_width] = grads[o * PAD : (o + 1) * PAD]
+
+    share = experts // far
+    for step in range(1, far + 1):
+        pl.loop(share * (step - 1), share * step if step < far else experts)(one_expert)
+        for way in range(2):
+            adapt_ring(step, way).wait()
+        if step < far:
+            for way in range(2):
+                adapt_ring(step + 1, way).start()
+        for offset in sorted({step, count - step}):
+            adapt_twin(offset).start()
+            adapt_sibling(offset, 0).start()
 
     def total(offset):
         return lax.dot_general(
@@ -277,6 +335,9 @@
             copy.start()
             later.append(copy)
         hops = later
+        for offset in (step - 1, count - step + 1):
+            adapt_twin(offset).wait()
+            adapt_sibling(offset, 1).start()
     result = total(0)
     for way in range(2):
         hops[way].wait()
@@ -284,7 +345,7 @@
     result = result.astype(jnp.bfloat16)
     token_out[...] = result
 
-    vis = visual_out.shape[0]
+    vis = shuffled_out.shape[0]
     row = lax.broadcasted_iota(jnp.int32, (vis, tokens), 0)
     theirs = (slot_row[...] == row + (1 - core) * vis).astype(jnp.bfloat16)
     vis_send[...] = jnp.dot(theirs, result, preferred_element_type=jnp.float32).astype(jnp.bfloat16)
@@ -292,30 +353,46 @@
         vis_send, vis_recv, v_send, v_recv, device_id=sibling, device_id_type=MESH
     )
     copy.start()
+    adapt_twin(far).wait()
+    adapt_sibling(far, 1).start()
     ours = (slot_row[...] == row + core * vis).astype(jnp.bfloat16)
     kept = jnp.dot(ours, result, preferred_element_type=jnp.float32)
     copy.wait()
-    visual_out[...] = (kept + vis_recv[...].astype(jnp.float32)).astype(jnp.bfloat16)
-
-
-def block_exchange(out_grad, gates, routes, tile_slot, w_in, w_out, expert_pre, vis_count):
+    visual = kept + vis_recv[...].astype(jnp.float32)
+    adapter = (visual * slope_in[...]).astype(jnp.bfloat16)
+    adapt_own.wait()
+    for offset in range(count):
+        for mine in range(2):
+            adapt_sibling(offset, mine).wait()
+    wide = 256
+    for begin in range(0, wa.shape[0], wide):
+        end = min(begin + wide, wa.shape[0])
+        shuffled_out[:, begin:end] = lax.dot_general(
+            adapter, wa[begin:end], (((1,), (1,)), ((), ())), preferred_element_type=jnp.float32
+        )
+
+
+def block_exchange(out_grad, gates, routes, tile_slot, w_in, w_out, expert_pre, adapter_pre, w_adapt):
     count = lax.axis_size("expert")
     tokens, width = out_grad.shape
     experts, fw, half_width = w_out.shape
     info = jnp.concatenate([gates.T, routes.T.astype(jnp.bfloat16)], axis=0)
     info = jnp.pad(info, ((0, PAD - 2 * TOP), (0, 0)))
+    vis_count = adapter_pre.shape[0]
+    outputs = w_adapt.shape[0] * count * 2
+    slope = gelu_slope(adapter_pre.astype(jnp.float32))
     slots = experts * PAD
     bf16 = jnp.bfloat16
     dma = pltpu.SemaphoreType.DMA
     far = count // 2
     vmem = pl.BlockSpec(memory_space=pltpu.VMEM)
-    token_grads, visual = pl.pallas_call(
+    return pl.pallas_call(
         exchange_kernel,
         out_shape=(
             jax.ShapeDtypeStruct((tokens, width), bf16),
-            jax.ShapeDtypeStruct((vis_count, width), bf16),
+            jax.ShapeDtypeStruct((vis_count, outputs), jnp.float32),
         ),
-        in_specs=[vmem] * 4 + [pl.BlockSpec(memory_space=pl.ANY)] * 2,
+        in_specs=[vmem] * 5 + [pl.BlockSpec(memory_space=pl.ANY)] * 3,
         out_specs=(vmem, vmem),
         scratch_shapes=[
             pltpu.VMEM((count, tokens, width), bf16),
@@ -331,36 +408,39 @@
             pltpu.VMEM((2, far, tokens, width), bf16),
             pltpu.VMEM((vis_count, width), bf16),
             pltpu.VMEM((vis_count, width), bf16),
+            pltpu.VMEM((outputs, width), bf16),
             dma((2, far + 1)), dma((2, far + 1)), dma((2, far + 1)), dma((2, far + 1)),
             dma((2, experts)), dma((2, experts)), dma((2, experts)),
             dma((2, far)), dma((2, far)), dma, dma,
+            dma, dma((2, far + 1)), dma((2, far + 1)), dma((count,)), dma((count,)), dma((2, count)), dma((2, count)),
         ],
         compiler_params=pltpu.CompilerParams(
-            collective_id=0, has_side_effects=True, vmem_limit_bytes=58 << 20
+            collective_id=0, has_side_effects=True, vmem_limit_bytes=61 << 20
         ),
         cost_estimate=pl.CostEstimate(
             flops=4 * experts * count * PAD * width * fw, bytes_accessed=4 * experts * width * fw, transcendentals=0
         ),
-    )(out_grad, info, tile_slot.reshape(1, tokens), expert_pre, w_out, w_in)
-    return token_grads, visual.astype(jnp.float32)
+    )(out_grad, info, tile_slot.reshape(1, tokens), expert_pre, slope, w_out, w_in, w_adapt)
 
 
 def body(out_grad, gates, routes, tile_slot, w_in, w_out, expert_pre, adapter_pre, w_adapt):
     vis_count = adapter_pre.shape[0]
-    if lax.axis_size("expert") == 8 and out_grad.shape[0] == 128 and expert_pre.shape[2] <= PAD:
-        exchange = block_exchange
+    sizes = (lax.axis_size("groups"), lax.axis_size("expert"), lax.axis_size("dp"))
+    if sizes == (2, 8, 2) and out_grad.shape[0] == 128 and expert_pre.shape[2] <= PAD:
+        token_grads, shuffled = block_exchange(
+            out_grad, gates, routes, tile_slot, w_in, w_out, expert_pre, adapter_pre, w_adapt
+        )
     else:
-        exchange = row_exchange
-    token_grads, visual_grad = exchange(
-        out_grad, gates, routes, tile_slot, w_in, w_out, expert_pre, vis_count
-    )
-    adapter_grad = (visual_grad * gelu_slope(adapter_pre.astype(jnp.float32))).astype(jnp.bfloat16)
-    shuffled = lax.dot_general(
-        adapter_grad,
-        lax.all_gather(w_adapt, ("expert", "dp"), axis=0, tiled=True),
-        (((1,), (1,)), ((), ())),
-        preferred_element_type=jnp.float32,
-    )
+        token_grads, visual_grad = row_exchange(
+            out_grad, gates, routes, tile_slot, w_in, w_out, expert_pre, vis_count
+        )
+        adapter_grad = (visual_grad * gelu_slope(adapter_pre.astype(jnp.float32))).astype(jnp.bfloat16)
+        shuffled = lax.dot_general(
+            adapter_grad,
+            lax.all_gather(w_adapt, ("expert", "dp"), axis=0, tiled=True),
+            (((1,), (1,)), ((), ())),
+            preferred_element_type=jnp.float32,
+        )
     tile_cols = vis_count // TILE_R
     patch_grads = shuffled.reshape(TILE_R, tile_cols, 2, 2, SIGW).transpose(0, 2, 1, 3, 4)
     patch_grads = patch_grads.reshape(2 * TILE_R, 2 * tile_cols * SIGW)

time: 138 us -> 104 us (0.75)
  Pallas kernels: 110 us -> 91.6 us
  between operations: 14.1 us -> 0.66 us
  matrix products: 4.69 us -> 0 us
  local copies, waits for them, and re-layouts: 5.7 us -> 7.72 us
  other arithmetic: 1.97 us -> 3.75 us
    pallas_call x1, Pallas kernels: 110 us -> 91.6 us  [block_exchange(): pl.pallas_call(exchange_kernel, out_shape=(jax.ShapeDtypeStruct((tokens,...]
    dot_general x1 -> x0, matrix products: 4.69 us -> none  [body(): lax.dot_general(adapter_grad, lax.all_gather(w_adapt, ('expert', 'dp'), a...]
    add x0 -> x1, other arithmetic: none -> 1.77 us  [gelu_slope(): normal_cdf + value * jnp.exp(-0.5 * value * value) * 0.3989422804014327]
    unnamed x6 -> x2, local copies, waits for them, and re-layouts: 3.54 us -> 4.52 us
  transfers between devices with their start and end apart: 1 -> 0, of which waited for: 0 -> 0; matrix products, arithmetic and copies ran while one was open for 3% -> 0% of each run, Pallas kernels for 80% -> 0%
where the time goes in v3:
time: 104 us
  Pallas kernels  91.6 us (88%)
  local copies, waits for them, and re-layouts  7.72 us (7%)
  other arithmetic  3.75 us (4%)
    pallas_call x1, Pallas kernels, block_exchange(): pl.pallas_call(exchange_kernel, out_shape=(jax.ShapeDtypeStruct((tokens,...  91.6 us
    unnamed x2, local copies, waits for them, and re-layouts  4.52 us

profile of v3, /device:TPU:0, one launch (start us, length us, event | category | flops | bytes accessed | tf_op | source)
XLA Modules:
  0.0 103.8 jit_solution(9011424868870161311)
XLA Ops:
  0.6 0.7 convert_bitcast_fusion
  1.3 1.3 %fusion.8.info = bf16[16,128]{1,0:T(8,128)(2,1)} fusion(bf16[6,128]{1,0:T(8,128)(2,1)S(1)} %convert_bitcast_fusion, bf16[6,128]{1,0:T(8,128)(2,1)} %bitcast.6), kind=kLoop, calls=%fused_computation.13 | loop fusion | flops 14336 | bytes 7168 | tf_op jit(solution)/shard_map/concatenate | solution.py:379
  2.6 1.8 %fusion.3.slope_in = f32[64,1280]{1,0:T(8,128)} fusion(bf16[64,1280]{1,0:T(8,128)(2,1)} %param.16), kind=kLoop, calls=%fused_computation.7 | loop fusion | flops 737280 | bytes 491520 | tf_op jit(solution)/shard_map/add | solution.py:21
  4.4 2.8 %copy.11.pre = bf16[8,8,14,768]{3,2,1,0:T(8,128)(2,1)} copy(bf16[8,8,14,768]{3,1,2,0:T(8,128)(2,1)} %param.15) | data formatting | bytes 2752512 | tf_op args[6]
  7.2 91.6 %shard_map.104 = (bf16[128,1280]{1,0:T(8,128)(2,1)}, f32[64,2304]{1,0:T(8,128)}) custom-call(bf16[128,1280]{1,0:T(8,128)(2,1)} %x.3, bf16[16,128]{1,0:T(8,128)(2,1)} %fusion.8.info, s32[1,128]{1,0:T(1,128)} %bitcast.7, bf16[8,8,14,768]{3,2,1,0:T(8,128)(2,1)} %copy.11.pre, f32[64,1280]{1,0:T(8,128)} %fusion.3.slope_in, bf16[8,768,640]{2,1,0:T(8,128)(2,1)} %w_out.1, ...), custom_call_target="tpu_custom_call" | custom-call | flops 4026531840 | bytes 31457280 | tf_op jit(solution)/shard_map/pallas_call | solution.py:389
  98.8 1.6 %reshape.14 = f32[8,8,2,2,576]{4,3,2,1,0:T(2,128)S(1)} reshape(f32[64,2304]{1,0:T(8,128)} %get-tuple-element.5) | data formatting | bytes 1179648 | tf_op jit(solution)/shard_map/reshape | solution.py:445
  100.4 0.1 copy.12
  100.5 1.5 %reshape.15 = f32[16,9216]{1,0:T(8,128)} reshape(f32[8,2,8,2,576]{4,3,2,1,0:T(2,128)S(1)} %copy.12) | data formatting | bytes 1179648 | tf_op jit(solution)/shard_map/reshape | solution.py:446
  102.1 1.7 %copy.14 = bf16[128,1280]{1,0:T(8,128)(2,1)} copy(bf16[128,1280]{1,0:T(8,128)(2,1)} %get-tuple-element.8) | data formatting | bytes 655360

commit v4 on v3

--- a/solution.py
+++ b/solution.py
@@ -108,7 +108,7 @@
 
 
 def exchange_kernel(
-    x, info, slot_row, pre, slope_in, w_out, w_in, w_adapt, token_out, shuffled_out,
+    x, info, slot_row, pre, slope_in, w_out, w_in, w_adapt, token_out, patch_out,
     xs, infos, wo, wi, placed, rows, back, scale, hidden, outbox, inbox, vis_send, vis_recv, wa,
     x_send, x_recv, i_send, i_recv, w_local, w_send, w_recv, r_send, r_recv, v_send, v_recv,
     a_own, a_send, a_recv, y_send, y_recv, s_send, s_recv,
@@ -345,7 +345,7 @@
     result = result.astype(jnp.bfloat16)
     token_out[...] = result
 
-    vis = shuffled_out.shape[0]
+    vis = slope_in.shape[0]
     row = lax.broadcasted_iota(jnp.int32, (vis, tokens), 0)
     theirs = (slot_row[...] == row + (1 - core) * vis).astype(jnp.bfloat16)
     vis_send[...] = jnp.dot(theirs, result, preferred_element_type=jnp.float32).astype(jnp.bfloat16)
@@ -364,12 +364,33 @@
     for offset in range(count):
         for mine in range(2):
             adapt_sibling(offset, mine).wait()
-    wide = 256
-    for begin in range(0, wa.shape[0], wide):
-        end = min(begin + wide, wa.shape[0])
-        shuffled_out[:, begin:end] = lax.dot_general(
-            adapter, wa[begin:end], (((1,), (1,)), ((), ())), preferred_element_type=jnp.float32
-        )
+    span = wa.shape[0] // 2
+    wide = 384
+    tile_cols = vis // TILE_R
+    deep = 2 * TILE_R
+    target = lax.broadcasted_iota(jnp.int32, (2 * vis, vis), 0)
+    origin = lax.broadcasted_iota(jnp.int32, (2 * vis, vis), 1)
+    spread = []
+    for y in range(2):
+        holds = (target % deep // 2 * tile_cols + target // deep == origin) & (target % 2 == y)
+        spread.append(
+            jnp.dot(
+                holds.astype(jnp.float32).astype(jnp.bfloat16), adapter, preferred_element_type=jnp.float32
+            ).astype(jnp.bfloat16)
+        )
+    for begin in range(0, span, wide):
+        size = min(wide, span - begin)
+        grads = sum(
+            lax.dot_general(
+                spread[y],
+                wa[y * span + begin : y * span + begin + size],
+                (((1,), (1,)), ((), ())),
+                preferred_element_type=jnp.float32,
+            )
+            for y in range(2)
+        )
+        for b in range(tile_cols):
+            patch_out[:, b * span + begin : b * span + begin + size] = grads[b * deep : (b + 1) * deep]
 
 
 def block_exchange(out_grad, gates, routes, tile_slot, w_in, w_out, expert_pre, adapter_pre, w_adapt):
@@ -390,7 +411,7 @@
         exchange_kernel,
         out_shape=(
             jax.ShapeDtypeStruct((tokens, width), bf16),
-            jax.ShapeDtypeStruct((vis_count, outputs), jnp.float32),
+            jax.ShapeDtypeStruct((2 * TILE_R, vis_count // TILE_R * outputs // 2), jnp.float32),
         ),
         in_specs=[vmem] * 5 + [pl.BlockSpec(memory_space=pl.ANY)] * 3,
         out_specs=(vmem, vmem),
@@ -427,20 +448,19 @@
     vis_count = adapter_pre.shape[0]
     sizes = (lax.axis_size("groups"), lax.axis_size("expert"), lax.axis_size("dp"))
     if sizes == (2, 8, 2) and out_grad.shape[0] == 128 and expert_pre.shape[2] <= PAD:
-        token_grads, shuffled = block_exchange(
+        return block_exchange(
             out_grad, gates, routes, tile_slot, w_in, w_out, expert_pre, adapter_pre, w_adapt
         )
-    else:
-        token_grads, visual_grad = row_exchange(
-            out_grad, gates, routes, tile_slot, w_in, w_out, expert_pre, vis_count
-        )
-        adapter_grad = (visual_grad * gelu_slope(adapter_pre.astype(jnp.float32))).astype(jnp.bfloat16)
-        shuffled = lax.dot_general(
-            adapter_grad,
-            lax.all_gather(w_adapt, ("expert", "dp"), axis=0, tiled=True),
-            (((1,), (1,)), ((), ())),
-            preferred_element_type=jnp.float32,
-        )
+    token_grads, visual_grad = row_exchange(
+        out_grad, gates, routes, tile_slot, w_in, w_out, expert_pre, vis_count
+    )
+    adapter_grad = (visual_grad * gelu_slope(adapter_pre.astype(jnp.float32))).astype(jnp.bfloat16)
+    shuffled = lax.dot_general(
+        adapter_grad,
+        lax.all_gather(w_adapt, ("expert", "dp"), axis=0, tiled=True),
+        (((1,), (1,)), ((), ())),
+        preferred_element_type=jnp.float32,
+    )
     tile_cols = vis_count // TILE_R
     patch_grads = shuffled.reshape(TILE_R, tile_cols, 2, 2, SIGW).transpose(0, 2, 1, 3, 4)
     patch_grads = patch_grads.reshape(2 * TILE_R, 2 * tile_cols * SIGW)

time: 104 us -> 103 us (level)
  local copies, waits for them, and re-layouts: 7.72 us -> 6.44 us
    reshape x2 -> x0, local copies, waits for them, and re-layouts: 3.12 us -> none  [the longest x1 1.59 us: body(): shuffled.reshape(TILE_R, tile_cols, 2, 2, SIGW).transpose(0, 2, 1, 3, 4)]
    unnamed x2 -> x3, local copies, waits for them, and re-layouts: 4.52 us -> 6.44 us
where the time goes in v4:
time: 103 us
  Pallas kernels  91.7 us (89%)
  local copies, waits for them, and re-layouts  6.44 us (6%)
  other arithmetic  3.75 us (4%)
    pallas_call x1, Pallas kernels, block_exchange(): pl.pallas_call(exchange_kernel, out_shape=(jax.ShapeDtypeStruct((tokens,...  91.7 us
    unnamed x3, local copies, waits for them, and re-layouts  6.44 us

profile of v4, /device:TPU:0, one launch (start us, length us, event | category | flops | bytes accessed | tf_op | source)
XLA Modules:
  0.0 102.5 jit_solution(3616319366081366843)
XLA Ops:
  0.6 0.7 convert_bitcast_fusion
  1.3 1.3 %fusion.8.info = bf16[16,128]{1,0:T(8,128)(2,1)} fusion(bf16[6,128]{1,0:T(8,128)(2,1)S(1)} %convert_bitcast_fusion, bf16[6,128]{1,0:T(8,128)(2,1)} %bitcast.4), kind=kLoop, calls=%fused_computation.13 | loop fusion | flops 14336 | bytes 7168 | tf_op jit(solution)/shard_map/concatenate | solution.py:400
  2.6 1.8 %fusion.3.slope_in = f32[64,1280]{1,0:T(8,128)} fusion(bf16[64,1280]{1,0:T(8,128)(2,1)} %param.16), kind=kLoop, calls=%fused_computation.7 | loop fusion | flops 737280 | bytes 491520 | tf_op jit(solution)/shard_map/add | solution.py:21
  4.4 2.8 %copy.11.pre = bf16[8,8,14,768]{3,2,1,0:T(8,128)(2,1)} copy(bf16[8,8,14,768]{3,1,2,0:T(8,128)(2,1)} %param.15) | data formatting | bytes 2752512 | tf_op args[6]
  7.2 91.7 %shard_map.104 = (bf16[128,1280]{1,0:T(8,128)(2,1)}, f32[16,9216]{1,0:T(8,128)}) custom-call(bf16[128,1280]{1,0:T(8,128)(2,1)} %x.3, bf16[16,128]{1,0:T(8,128)(2,1)} %fusion.8.info, s32[1,128]{1,0:T(1,128)} %bitcast.5, bf16[8,8,14,768]{3,2,1,0:T(8,128)(2,1)} %copy.11.pre, f32[64,1280]{1,0:T(8,128)} %fusion.3.slope_in, bf16[8,768,640]{2,1,0:T(8,128)(2,1)} %w_out.1, ...), custom_call_target="tpu_custom_call" | custom-call | flops 4026531840 | bytes 31457280 | tf_op jit(solution)/shard_map/pallas_call | solution.py:410
  98.9 1.7 %copy.14 = bf16[128,1280]{1,0:T(8,128)(2,1)} copy(bf16[128,1280]{1,0:T(8,128)(2,1)} %get-tuple-element.4) | data formatting | bytes 655360
  100.6 1.9 %copy.15 = f32[16,9216]{1,0:T(8,128)} copy(f32[16,9216]{1,0:T(8,128)} %get-tuple-element.5) | data formatting | bytes 1179648

commit v5 on v4

--- a/solution.py
+++ b/solution.py
@@ -186,26 +186,23 @@
         block = x if step == 1 else xs.at[come]
         note = info if step == 1 else infos.at[come]
         to = (right, left)[way]
-        copies = []
-        at = pl.ds(way * half, half) if step == far else pl.ds(0, tokens)
-        copies.append(
-            pltpu.make_async_remote_copy(
-                block.at[at], xs.at[go, at], x_send.at[way, step], x_recv.at[way, step],
+        copies = {}
+        for part in (0, 1) if step < far else (way,):
+            at = pl.ds(part * half, half)
+            copies[part] = pltpu.make_async_remote_copy(
+                block.at[at], xs.at[go, at], x_send.at[way, step, part], x_recv.at[way, step, part],
                 device_id=to, device_id_type=MESH,
             )
-        )
         if step < far or way == 0:
-            copies.append(
-                pltpu.make_async_remote_copy(
-                    note, infos.at[go], i_send.at[way, step], i_recv.at[way, step],
-                    device_id=to, device_id_type=MESH,
-                )
+            copies[2] = pltpu.make_async_remote_copy(
+                note, infos.at[go], i_send.at[way, step], i_recv.at[way, step],
+                device_id=to, device_id_type=MESH,
             )
         return copies
 
     sends = [ring(1, 0), ring(1, 1)]
     for copies in sends:
-        for copy in copies:
+        for copy in copies.values():
             copy.start()
 
     @pl.loop(0, experts)
@@ -245,15 +242,15 @@
 
     take(0)
     for step in range(1, far + 1):
-        for copies in sends:
-            for copy in copies:
-                copy.wait()
-        if step < far:
-            sends = [ring(step + 1, 0), ring(step + 1, 1)]
-            for copies in sends:
-                for copy in copies:
-                    copy.start()
-        else:
+        later = [ring(step + 1, way) if step < far else {} for way in range(2)]
+        for part in range(3):
+            for way in range(2):
+                if part in sends[way]:
+                    sends[way][part].wait()
+                if part in later[way]:
+                    later[way][part].start()
+        sends = later
+        if step == far:
             for way in range(2):
                 adapt_ring(1, way).start()
         take(step)
@@ -430,7 +427,7 @@
             pltpu.VMEM((vis_count, width), bf16),
             pltpu.VMEM((vis_count, width), bf16),
             pltpu.VMEM((outputs, width), bf16),
-            dma((2, far + 1)), dma((2, far + 1)), dma((2, far + 1)), dma((2, far + 1)),
+            dma((2, far + 1, 2)), dma((2, far + 1, 2)), dma((2, far + 1)), dma((2, far + 1)),
             dma((2, experts)), dma((2, experts)), dma((2, experts)),
             dma((2, far)), dma((2, far)), dma, dma,
             dma, dma((2, far + 1)), dma((2, far + 1)), dma((count,)), dma((count,)), dma((2, count)), dma((2, count)),

time: 103 us -> 103 us (level)
  no operation moved by 1% of the time
where the time goes in v5:
time: 103 us
  Pallas kernels  91.9 us (89%)
  local copies, waits for them, and re-layouts  6.44 us (6%)
  other arithmetic  3.75 us (4%)
    pallas_call x1, Pallas kernels, block_exchange(): pl.pallas_call(exchange_kernel, out_shape=(jax.ShapeDtypeStruct((tokens,...  91.9 us
    unnamed x3, local copies, waits for them, and re-layouts  6.44 us

profile of v5, /device:TPU:0, one launch (start us, length us, event | category | flops | bytes accessed | tf_op | source)
XLA Modules:
  0.0 102.7 jit_solution(6581428052556988126)
XLA Ops:
  0.6 0.7 convert_bitcast_fusion
  1.3 1.3 %fusion.8.info = bf16[16,128]{1,0:T(8,128)(2,1)} fusion(bf16[6,128]{1,0:T(8,128)(2,1)S(1)} %convert_bitcast_fusion, bf16[6,128]{1,0:T(8,128)(2,1)} %bitcast.4), kind=kLoop, calls=%fused_computation.13 | loop fusion | flops 14336 | bytes 7168 | tf_op jit(solution)/shard_map/concatenate | solution.py:397
  2.6 1.8 %fusion.3.slope_in = f32[64,1280]{1,0:T(8,128)} fusion(bf16[64,1280]{1,0:T(8,128)(2,1)} %param.16), kind=kLoop, calls=%fused_computation.7 | loop fusion | flops 737280 | bytes 491520 | tf_op jit(solution)/shard_map/add | solution.py:21
  4.4 2.8 %copy.11.pre = bf16[8,8,14,768]{3,2,1,0:T(8,128)(2,1)} copy(bf16[8,8,14,768]{3,1,2,0:T(8,128)(2,1)} %param.15) | data formatting | bytes 2752512 | tf_op args[6]
  7.2 91.9 %shard_map.104 = (bf16[128,1280]{1,0:T(8,128)(2,1)}, f32[16,9216]{1,0:T(8,128)}) custom-call(bf16[128,1280]{1,0:T(8,128)(2,1)} %x.3, bf16[16,128]{1,0:T(8,128)(2,1)} %fusion.8.info, s32[1,128]{1,0:T(1,128)} %bitcast.5, bf16[8,8,14,768]{3,2,1,0:T(8,128)(2,1)} %copy.11.pre, f32[64,1280]{1,0:T(8,128)} %fusion.3.slope_in, bf16[8,768,640]{2,1,0:T(8,128)(2,1)} %w_out.1, ...), custom_call_target="tpu_custom_call" | custom-call | flops 4026531840 | bytes 31457280 | tf_op jit(solution)/shard_map/pallas_call | solution.py:407
  99.1 1.7 %copy.14 = bf16[128,1280]{1,0:T(8,128)(2,1)} copy(bf16[128,1280]{1,0:T(8,128)(2,1)} %get-tuple-element.4) | data formatting | bytes 655360
  100.8 1.9 %copy.15 = f32[16,9216]{1,0:T(8,128)} copy(f32[16,9216]{1,0:T(8,128)} %get-tuple-element.5) | data formatting | bytes 1179648
